TPU v7x, 32 devices: a whole 2x2x4 slice. The times are simulated.
32 devices in a mesh: group: 2 (over y), row: 2 (over core), col: 8 (over z, x).
Axes of the slice: x: 2, y: 2, z: 4, core: 2. Of those that a mesh axis runs over, the one named last changes fastest.
Arguments:
- tokens: bfloat16 [1024, 8192], P(('group', 'col'), 'row'), parts along dimension 0, may hold values from -6 to 6
- cotangent: bfloat16 [1024, 8192], P(('group', 'col'), 'row'), parts along dimension 0, may hold values from -6 to 6
- gate_weight: bfloat16 [8192, 16384], P('row', 'col'), may hold values from -0.09375 to 0.09375
- up_weight: bfloat16 [8192, 16384], P('row', 'col'), may hold values from -0.09375 to 0.09375
- down_weight: bfloat16 [16384, 8192], P('col', 'row'), may hold values from -0.0625 to 0.0625
- gate_mask: int32 [64, 128], P('row', 'col'), may hold values from 0 to 1, as said below
- up_mask: int32 [64, 128], P('row', 'col'), may hold values from 0 to 1, as said below
- down_mask: int32 [128, 64], P('col', 'row'), may hold values from 0 to 1, as said below
Outputs:
- output: bfloat16 [1024, 8192], P(('group', 'col'), 'row'), parts along dimension 0
- input_grad: bfloat16 [1024, 8192], P(('group', 'col'), 'row'), parts along dimension 0
- gate_grad: bfloat16 [16384, 16384], P(('group', 'row'), 'col'), parts along dimension 0
- up_grad: bfloat16 [16384, 16384], P(('group', 'row'), 'col'), parts along dimension 0
- down_grad: bfloat16 [32768, 8192], P(('group', 'col'), 'row'), parts along dimension 0
There are 2 independent parts, one for each index of `group`. A program takes and returns all parts, laid end to end along the dimension named above; an argument that names none is the same for every part. Nothing has to cross between parts.
Inputs may be any that keep to these rules, and one draw needn't show every extreme that they name: `gate_mask`: 1 keeps a 128 x 128 block of the projection, 0 removes it. `up_mask`: 1 keeps a 128 x 128 block of the projection, 0 removes it. `down_mask`: 1 keeps a 128 x 128 block of the projection, 0 removes it.
All inputs are finite; a program needn't handle non-finite values.
Results may differ from a plain program's by a relative error of at most 0.005.
Values may be sent and summed in bfloat16 or wider, within the bound.
A program may use at most 320 MiB of HBM per device.

v0:
```python
import jax
import jax.numpy as jnp
from jax import lax
from jax.sharding import PartitionSpec as P

BLOCK = 128


def spread(block_mask):
    row_blocks, col_blocks = block_mask.shape
    expanded = jnp.broadcast_to(
        block_mask.astype(jnp.bfloat16)[:, None, :, None], (row_blocks, BLOCK, col_blocks, BLOCK)
    )
    return expanded.reshape(row_blocks * BLOCK, col_blocks * BLOCK)


def contract_rows(left, right):
    return lax.dot_general(
        left, right, (((0,), (0,)), ((), ())), preferred_element_type=jnp.float32
    )


def body(tokens, cotangent, gate_weight, up_weight, down_weight, gate_mask, up_mask, down_mask):
    gate_keep = spread(gate_mask)
    up_keep = spread(up_mask)
    down_keep = spread(down_mask)
    both_eff = jnp.concatenate([gate_weight * gate_keep, up_weight * up_keep], axis=1)
    down_eff = down_weight * down_keep
    hidden_cols = gate_weight.shape[1]
    gathered = lax.all_gather(tokens, "col", axis=0, tiled=True)
    partial_sums = lax.psum(jnp.dot(gathered, both_eff, preferred_element_type=jnp.float32), "row")
    gate_pre = partial_sums[:, :hidden_cols]
    up_pre = partial_sums[:, hidden_cols:]
    sigmoid_gate = jax.nn.sigmoid(gate_pre)
    activated = gate_pre * sigmoid_gate
    hidden = (activated * up_pre).astype(jnp.bfloat16)
    row_block = hidden
    output = lax.psum_scatter(
        jnp.dot(row_block, down_eff, preferred_element_type=jnp.float32),
        "col",
        scatter_dimension=0,
        tiled=True,
    ).astype(jnp.bfloat16)
    shard_rows = lax.all_gather(cotangent, "col", axis=0, tiled=True)
    term = lax.dot_general(
        shard_rows, down_eff, (((1,), (1,)), ((), ())), preferred_element_type=jnp.float32
    )
    row_block = hidden
    down_total = contract_rows(row_block, shard_rows)
    hidden_grad = lax.psum(term, "row")
    gate_delta = (
        hidden_grad * up_pre * sigmoid_gate * (1.0 + gate_pre * (1.0 - sigmoid_gate))
    ).astype(jnp.bfloat16)
    up_delta = (hidden_grad * activated).astype(jnp.bfloat16)
    both_delta = jnp.concatenate([gate_delta, up_delta], axis=1)
    row_block = both_delta
    input_grad = lax.psum_scatter(
        lax.dot_general(
            row_block, both_eff, (((1,), (1,)), ((), ())), preferred_element_type=jnp.float32
        ),
        "col",
        scatter_dimension=0,
        tiled=True,
    ).astype(jnp.bfloat16)
    features = lax.all_gather(tokens, "col", axis=0, tiled=True)
    gate_grad = (contract_rows(features, gate_delta) * gate_keep).astype(jnp.bfloat16)
    up_grad = (contract_rows(features, up_delta) * up_keep).astype(jnp.bfloat16)
    down_grad = (down_total * down_keep).astype(jnp.bfloat16)
    return (output, input_grad, gate_grad, up_grad, down_grad)


def solution(mesh):
    in_specs = (
        P(("group", "col"), "row"),
        P(("group", "col"), "row"),
        P("row", "col"),
        P("row", "col"),
        P("col", "row"),
        P("row", "col"),
        P("row", "col"),
        P("col", "row"),
    )
    out_specs = (
        P(("group", "col"), "row"),
        P(("group", "col"), "row"),
        P(("group", "row"), "col"),
        P(("group", "row"), "col"),
        P(("group", "col"), "row"),
    )
    return jax.shard_map(body, mesh=mesh, in_specs=in_specs, out_specs=out_specs, check_vma=False)
```

profile of v0, /device:TPU:0, one launch (start us, length us, event | category | flops | bytes accessed | tf_op | source)
XLA Modules:
  0.0 578.8 jit_solution(12022222742906459888)
XLA Ops:
  7.2 0.0 all-gather.5.cloned.1.call-start
  7.2 0.7 all-gather.5.cloned.1.call-update
  7.9 0.0 all-gather.3.cloned.1.call-start
  7.9 0.7 all-gather.3.cloned.1.call-update
  8.6 0.0 all-reduce.3.cloned.1.call-start
  8.7 0.7 convert_element_type.42
  9.4 0.7 convert_element_type.43
  10.1 0.7 convert_element_type.45
  10.8 21.2 %copy.13 = bf16[4096,2048]{0,1:T(8,128)(2,1)} copy(bf16[4096,2048]{1,0:T(8,128)(2,1)} %param.10) | data formatting | bytes 33554432 | tf_op args[2]
  32.0 21.4 %copy.14 = bf16[4096,2048]{0,1:T(8,128)(2,1)} copy(bf16[4096,2048]{1,0:T(8,128)(2,1)} %param.11) | data formatting | bytes 33554432 | tf_op args[3]
  53.5 6.2 %broadcast_in_dim.7 = bf16[32,128,16,128]{1,0,3,2:T(8,128)(2,1)} broadcast(bf16[32,16]{0,1:T(8,128)(2,1)S(1)} %convert_element_type.43), dimensions={0,2} | broadcast | bytes 16778240 | tf_op jit(solution)/shard_map/broadcast_in_dim | solution.py:11
  59.7 2.8 broadcast_in_dim.6
  62.5 0.0 copy-start
  62.5 5.7 copy-done
  68.2 30.1 %bitcast_multiply_fusion.3 = (bf16[4096,2048]{0,1:T(8,128)(2,1)}, bf16[4096,2048]{0,1:T(8,128)(2,1)}) fusion(bf16[4096,2048]{0,1:T(8,128)(2,1)} %copy.14, bf16[256,8,32,128]{3,2,1,0:T(8,128)(2,1)} %bitcast.46, bf16[4096,2048]{0,1:T(8,128)(2,1)} %copy.13, bf16[256,8,32,128]{3,2,1,0:T(8,128)(2,1)S(1)} %bitcast.44), kind=kLoop, calls=%fused_computation.9 | loop fusion | flops 16777216 | bytes 100663296 | tf_op jit(solution)/shard_map/mul | solution.py:27
  98.3 0.0 all-gather.5.cloned.1.call-done
  98.3 6.3 %broadcast_in_dim.8 = bf16[16,128,32,128]{3,2,1,0:T(8,128)(2,1)} broadcast(bf16[16,32]{1,0:T(8,128)(2,1)S(1)} %convert_element_type.45), dimensions={0,2} | broadcast | bytes 16778240 | tf_op jit(solution)/shard_map/broadcast_in_dim | solution.py:11
  104.6 19.3 %fusion.11 = f32[512,2048]{0,1:T(8,128)} fusion(bf16[512,4096]{1,0:T(8,128)(2,1)} %all-gather.5.cloned.1.call-done, bf16[2048,4096]{1,0:T(8,128)(2,1)} %param.12, bf16[256,8,32,128]{3,2,1,0:T(8,128)(2,1)} %bitcast.48), kind=kOutput, calls=%fused_computation.22 | convolution fusion | flops 8598323200 | bytes 41943040 | tf_op jit(solution)/shard_map/dot_general | solution.py:45
  123.9 36.2 %all-gather.3.cloned.1.call-done = bf16[512,4096]{1,0:T(8,128)(2,1)} async-done(((bf16[64,4096]{1,0:T(8,128)(2,1)}), bf16[512,4096]{1,0:T(8,128)(2,1)}) %all-gather.3.cloned.1.call-update) | async-done | bytes 4194320 | tf_op jit(solution)/shard_map/all_gather | solution.py:30
  160.1 24.8 %fusion.4 = f32[512,4096]{0,1:T(8,128)} fusion(bf16[512,4096]{1,0:T(8,128)(2,1)} %all-gather.3.cloned.1.call-done, bf16[4096,2048]{0,1:T(8,128)(2,1)} %get-tuple-element.15, bf16[4096,2048]{0,1:T(8,128)(2,1)} %get-tuple-element.16), kind=kOutput, calls=%fused_computation.11 | convolution fusion | flops 17246978048 | bytes 46137344 | tf_op jit(solution)/shard_map/dot_general | solution.py:31
  184.9 0.0 all-reduce.3.cloned.1.call-update
  184.9 0.0 reduce-scatter.5.cloned.1.call-start
  185.0 47.9 %all-reduce.3.cloned.1.call-done = (f32[512,4096]{0,1:T(8,128)}, f32[512,2048]{0,1:T(8,128)}) async-done(((f32[512,4096]{0,1:T(8,128)}, f32[512,2048]{0,1:T(8,128)}), (f32[512,4096]{0,1:T(8,128)}, f32[512,2048]{0,1:T(8,128)})) %all-reduce.3.cloned.1.call-update) | async-done | bytes 12582928 | tf_op jit(solution)/shard_map/psum | solution.py:31
  232.8 7.4 %multiply_convert_fusion.2 = (bf16[512,2048]{0,1:T(8,128)(2,1)}, bf16[512,2048]{0,1:T(8,128)(2,1)}, bf16[512,2048]{0,1:T(8,128)(2,1)S(1)}) fusion(f32[512,2048]{0,1:T(8,128)} %get-tuple-element.11, f32[512,4096]{0,1:T(8,128)} %get-tuple-element.10), kind=kLoop, calls=%fused_computation.18 | loop fusion | flops 15728640 | bytes 18874368 | tf_op jit(solution)/shard_map/convert_element_type | solution.py:53
  240.3 27.4 %fusion.2 = f32[512,4096]{1,0:T(8,128)} fusion(bf16[4096,2048]{0,1:T(8,128)(2,1)} %get-tuple-element.15, bf16[4096,2048]{0,1:T(8,128)(2,1)} %get-tuple-element.16, bf16[512,2048]{0,1:T(8,128)(2,1)} %get-tuple-element.13, bf16[512,2048]{0,1:T(8,128)(2,1)} %get-tuple-element.12), kind=kOutput, calls=%fused_computation.6 | convolution fusion | flops 17255366656 | bytes 46137344 | tf_op jit(solution)/shard_map/dot_general | solution.py:58
  267.7 0.0 reduce-scatter.5.cloned.1.call-update
  267.7 0.0 reduce-scatter.3.cloned.1.call-start
  267.8 18.2 %fusion.6 = f32[512,4096]{1,0:T(8,128)} fusion(bf16[512,2048]{0,1:T(8,128)(2,1)S(1)} %get-tuple-element.14, bf16[2048,4096]{1,0:T(8,128)(2,1)} %param.12, bf16[256,8,32,128]{3,2,1,0:T(8,128)(2,1)} %bitcast.49), kind=kOutput, calls=%fused_computation.13 | convolution fusion | flops 8598323200 | bytes 44040192 | tf_op jit(solution)/shard_map/dot_general | solution.py:39
  285.9 0.0 reduce-scatter.3.cloned.1.call-update
  285.9 19.2 %fusion = bf16[4096,2048]{0,1:T(8,128)(2,1)} fusion(bf16[512,2048]{0,1:T(8,128)(2,1)} %get-tuple-element.13, bf16[512,4096]{1,0:T(8,128)(2,1)} %all-gather.3.cloned.1.call-done, bf16[256,8,32,128]{3,2,1,0:T(8,128)(2,1)} %bitcast.47), kind=kOutput, calls=%fused_computation.2 | convolution fusion | flops 8615100416 | bytes 39845888 | tf_op jit(solution)/shard_map/dot_general | solution.py:18
  305.2 22.5 %copy.16 = bf16[4096,2048]{1,0:T(8,128)(2,1)} copy(bf16[4096,2048]{0,1:T(8,128)(2,1)} %fusion) | data formatting | bytes 33554432
  327.7 19.5 %fusion.1 = bf16[4096,2048]{0,1:T(8,128)(2,1)} fusion(bf16[512,2048]{0,1:T(8,128)(2,1)} %get-tuple-element.12, bf16[512,4096]{1,0:T(8,128)(2,1)} %all-gather.3.cloned.1.call-done, bf16[256,8,32,128]{3,2,1,0:T(8,128)(2,1)} %bitcast.45), kind=kOutput, calls=%fused_computation.4 | convolution fusion | flops 8615100416 | bytes 39845888 | tf_op jit(solution)/shard_map/dot_general | solution.py:18
  347.2 22.5 %copy.15 = bf16[4096,2048]{1,0:T(8,128)(2,1)} copy(bf16[4096,2048]{0,1:T(8,128)(2,1)} %fusion.1) | data formatting | bytes 33554432
  369.7 18.6 %multiply_convert_fusion = bf16[2048,4096]{1,0:T(8,128)(2,1)} fusion(bf16[512,2048]{0,1:T(8,128)(2,1)S(1)} %get-tuple-element.14, bf16[512,4096]{1,0:T(8,128)(2,1)} %all-gather.5.cloned.1.call-done, bf16[256,8,32,128]{3,2,1,0:T(8,128)(2,1)} %bitcast.50), kind=kOutput, calls=%fused_computation.5 | convolution fusion | flops 8615100416 | bytes 39845888 | tf_op jit(solution)/shard_map/dot_general | solution.py:18
  388.4 29.6 %reduce-scatter.5.cloned.1.call-done = f32[64,4096]{1,0:T(8,128)} async-done(((f32[512,4096]{1,0:T(8,128)}), f32[64,4096]{1,0:T(8,128)}) %reduce-scatter.5.cloned.1.call-update) | async-done | bytes 1048592 | tf_op jit(solution)/shard_map/reduce_scatter | solution.py:57
  417.9 2.1 convert_element_type.49
  420.0 150.0 %reduce-scatter.3.cloned.1.call-done = f32[64,4096]{1,0:T(8,128)} async-done(((f32[512,4096]{1,0:T(8,128)}), f32[64,4096]{1,0:T(8,128)}) %reduce-scatter.3.cloned.1.call-update) | async-done | bytes 1048592 | tf_op jit(solution)/shard_map/reduce_scatter | solution.py:38
  570.0 2.1 convert_element_type.46
Async XLA Ops:
  7.2 91.2 %all-gather.5.cloned.1.call-start = ((), (), s32[]{:S(2)}) async-start(), calls=%async_computation.4 | async-start | bytes 4718592 | tf_op jit(solution)/shard_map/all_gather | solution.py:44
  7.9 152.2 %all-gather.3.cloned.1.call-start = ((), (), s32[]{:S(2)}) async-start(), calls=%async_computation.2 | async-start | bytes 4718592 | tf_op jit(solution)/shard_map/all_gather | solution.py:30
  8.6 224.2 %all-reduce.3.cloned.1.call-start = ((), (), s32[]{:S(2)}) async-start(), calls=%async_computation.6 | async-start | bytes 25165824 | tf_op jit(solution)/shard_map/psum | solution.py:31
  62.5 5.7 copy-start
  184.9 233.0 %reduce-scatter.5.cloned.1.call-start = ((), (), s32[]{:S(2)}) async-start(), calls=%async_computation.5 | async-start | bytes 9437184 | tf_op jit(solution)/shard_map/reduce_scatter | solution.py:57
  267.7 302.3 %reduce-scatter.3.cloned.1.call-start = ((), (), s32[]{:S(2)}) async-start(), calls=%async_computation.3 | async-start | bytes 9437184 | tf_op jit(solution)/shard_map/reduce_scatter | solution.py:38
Sparse Core Ops, SparseCore 0:
  10.1 76.0 all-gather.4
  88.4 71.6 all-gather.2
  185.0 47.7 all-reduce.2
  267.8 150.0 reduce-scatter.4
  421.9 148.0 reduce-scatter.2
where the time goes:
time: 588 us; the launch traced here: 579 us
  waiting for transfers between devices  265 us (45%)
  matrix products  147 us (25%)
  local copies, waits for them, and re-layouts  109 us (19%)
  other arithmetic  43.8 us (7%)
  between operations  14 us (2%)
    reduce_scatter x1, waiting for transfers between devices, body(): lax.psum_scatter(jnp.dot(row_block, down_eff, preferred_element_type=jnp....  150 us
    unnamed x6, local copies, waits for them, and re-layouts  93.4 us
    dot_general x3, matrix products, contract_rows(): lax.dot_general(left, right, (((0,), (0,)), ((), ())), preferred_element_...  57.4 us
    psum x1, waiting for transfers between devices, body(): lax.psum(jnp.dot(gathered, both_eff, preferred_element_type=jnp.float32),...  47.9 us
    all_gather x1, waiting for transfers between devices, body(): gathered = lax.all_gather(tokens, 'col', axis=0, tiled=True)  36.2 us
    mul x1, other arithmetic, body(): up_weight * up_keep  30.1 us
    reduce_scatter x1, waiting for transfers between devices, body(): lax.psum_scatter(lax.dot_general(row_block, both_eff, (((1,), (1,)), ((),...  29.6 us
    dot_general x1, matrix products, body(): lax.dot_general(row_block, both_eff, (((1,), (1,)), ((), ())), preferred_...  27.4 us
  transfers between devices with their start and end apart: 5, of which 4 were waited for; matrix products, arithmetic and copies ran while one was open for 40% of the time, Pallas kernels for 0%

commit v1 on v0

--- a/solution.py
+++ b/solution.py
@@ -2,6 +2,7 @@
 import jax.numpy as jnp
 from jax import lax
 from jax.sharding import PartitionSpec as P
+from jax.lax import axis_index, axis_size, ppermute
 
 BLOCK = 128
 
@@ -27,7 +28,33 @@
     both_eff = jnp.concatenate([gate_weight * gate_keep, up_weight * up_keep], axis=1)
     down_eff = down_weight * down_keep
     hidden_cols = gate_weight.shape[1]
-    gathered = lax.all_gather(tokens, "col", axis=0, tiled=True)
+    arr_next, part_now, main = (axis_size("col"), axis_index("col"), tokens.shape[0])
+    pool = []
+    ix = 0
+    while ix < arr_next:
+        pool.append((ix, (ix + 1) % arr_next))
+        ix = ix + 1
+    entries = []
+    ix = 0
+    while ix < arr_next:
+        entries.append((ix, (ix - 1) % arr_next))
+        ix += 1
+    gathered = jnp.zeros((*tokens.shape[:0], arr_next * main, *tokens.shape[0 + 1 :]), tokens.dtype)
+    gathered = lax.dynamic_update_slice_in_dim(gathered, tokens, part_now * main, axis=0)
+    arr_now = high = tokens
+    frame_out = arr_next // 2
+    i = 1
+    while i < frame_out + 1:
+        arr_now = ppermute(arr_now, "col", pool)
+        gathered = lax.dynamic_update_slice_in_dim(
+            gathered, arr_now, (part_now - i) % arr_next * main, axis=0
+        )
+        if i < arr_next - frame_out:
+            high = ppermute(high, "col", perm=entries)
+            gathered = lax.dynamic_update_slice_in_dim(
+                gathered, high, (part_now + i) % arr_next * main, axis=0
+            )
+        i += 1
     partial_sums = lax.psum(jnp.dot(gathered, both_eff, preferred_element_type=jnp.float32), "row")
     gate_pre = partial_sums[:, :hidden_cols]
     up_pre = partial_sums[:, hidden_cols:]

time: 588 us -> 661 us (1.12)
  waiting for transfers between devices: 265 us -> 296 us
  starting transfers between devices: 0.2 us -> 28.9 us
  matrix products: 147 us -> 158 us
  local copies, waits for them, and re-layouts: 109 us -> 117 us
    reduce_scatter x1, waiting for transfers between devices: 29.6 us -> 150 us  [body(): lax.psum_scatter(lax.dot_general(row_block, both_eff, (((1,), (1,)), ((),...]
    reduce_scatter x1, waiting for transfers between devices: 150 us -> 38.1 us  [body(): lax.psum_scatter(jnp.dot(row_block, down_eff, preferred_element_type=jnp....]
    ppermute x0 -> x7, waiting for transfers between devices: none -> 35 us  [the longest x4 34.9 us: body(): arr_now = ppermute(arr_now, 'col', pool)]
    ppermute x0 -> x7, starting transfers between devices: none -> 28.5 us  [the longest x3 20.1 us: body(): high = ppermute(high, 'col', perm=entries)]
    all_gather x1, waiting for transfers between devices: 36.2 us -> 24.2 us  [body(): features = lax.all_gather(tokens, 'col', axis=0, tiled=True)]
    dot_general x3, matrix products: 57.4 us -> 67.7 us  [contract_rows(): lax.dot_general(left, right, (((0,), (0,)), ((), ())), preferred_element_...]
    dynamic_update_slice x0 -> x8, local copies, waits for them, and re-layouts: none -> 6.66 us  [the longest x4 3.32 us: body(): lax.dynamic_update_slice_in_dim(gathered, arr_now, (part_now - i) % arr_n...]
    unnamed x6 -> x14, local copies, waits for them, and re-layouts: 93.4 us -> 91.1 us
  transfers between devices with their start and end apart: 5 -> 12, of which waited for: 4 -> 7; matrix products, arithmetic and copies ran while one was open for 40% -> 43% of each run, Pallas kernels for 0% -> 0%
where the time goes in v1:
time: 661 us; the launch traced here: 655 us
  waiting for transfers between devices  296 us (45%)
  matrix products  158 us (24%)
  local copies, waits for them, and re-layouts  117 us (18%)
  other arithmetic  41.8 us (6%)
  starting transfers between devices  28.9 us (4%)
  between operations  14.1 us (2%)
    reduce_scatter x1, waiting for transfers between devices, body(): lax.psum_scatter(lax.dot_general(row_block, both_eff, (((1,), (1,)), ((),...  150 us
    unnamed x14, local copies, waits for them, and re-layouts  91.1 us
    dot_general x3, matrix products, contract_rows(): lax.dot_general(left, right, (((0,), (0,)), ((), ())), preferred_element_...  67.7 us
    psum x1, waiting for transfers between devices, body(): lax.psum(jnp.dot(gathered, both_eff, preferred_element_type=jnp.float32),...  47.7 us
    reduce_scatter x1, waiting for transfers between devices, body(): lax.psum_scatter(jnp.dot(row_block, down_eff, preferred_element_type=jnp....  38.1 us
    ppermute x4, waiting for transfers between devices, body(): arr_now = ppermute(arr_now, 'col', pool)  34.9 us
    mul x1, other arithmetic, body(): up_weight * up_keep  30.1 us
    dot_general x1, matrix products, body(): lax.dot_general(row_block, both_eff, (((1,), (1,)), ((), ())), preferred_...  27.1 us
  transfers between devices with their start and end apart: 12, of which 7 were waited for; matrix products, arithmetic and copies ran while one was open for 43% of the time, Pallas kernels for 0%

profile of v1, /device:TPU:0, one launch (start us, length us, event | category | flops | bytes accessed | tf_op | source)
XLA Modules:
  0.0 654.7 jit_solution(147431393244426089)
XLA Ops:
  7.2 0.0 all-gather.3.cloned.1.call-start
  7.2 3.0 collective-permute-start
  10.2 3.1 collective-permute-start.1
  13.3 0.0 all-gather.3.cloned.1.call-update
  13.3 0.0 all-reduce.3.cloned.1.call-start
  13.4 21.3 %copy.14 = bf16[4096,2048]{0,1:T(8,128)(2,1)} copy(bf16[4096,2048]{1,0:T(8,128)(2,1)} %param.11) | data formatting | bytes 33554432 | tf_op args[3]
  34.7 21.4 %copy.13 = bf16[4096,2048]{0,1:T(8,128)(2,1)} copy(bf16[4096,2048]{1,0:T(8,128)(2,1)} %param.10) | data formatting | bytes 33554432 | tf_op args[2]
  56.1 2.8 broadcast_in_dim.10
  59.0 7.4 %broadcast_in_dim.9 = bf16[32,128,16,128]{1,0,3,2:T(8,128)(2,1)} broadcast(bf16[32,16]{0,1:T(8,128)(2,1)S(1)} %convert_element_type.42), dimensions={0,2} | broadcast | bytes 16778240 | tf_op jit(solution)/shard_map/broadcast_in_dim | solution.py:12
  66.4 3.3 copy-done
  69.7 30.1 %bitcast_multiply_fusion.3 = (bf16[4096,2048]{0,1:T(8,128)(2,1)}, bf16[4096,2048]{0,1:T(8,128)(2,1)}) fusion(bf16[4096,2048]{0,1:T(8,128)(2,1)} %copy.14, bf16[256,8,32,128]{3,2,1,0:T(8,128)(2,1)S(1)} %bitcast.42, bf16[4096,2048]{0,1:T(8,128)(2,1)} %copy.13, bf16[256,8,32,128]{3,2,1,0:T(8,128)(2,1)} %bitcast.44), kind=kLoop, calls=%fused_computation.9 | loop fusion | flops 16777216 | bytes 100663296 | tf_op jit(solution)/shard_map/mul | solution.py:28
  99.9 2.4 broadcast_in_dim.8
  102.3 0.8 constant_dynamic-update-slice_fusion.7
  103.2 4.7 collective-permute-start.3
  107.9 0.8 constant_dynamic-update-slice_fusion.6
  108.7 0.8 constant_dynamic-update-slice_fusion.5
  109.5 16.0 %collective-permute-done.2 = bf16[64,4096]{1,0:T(8,128)(2,1)S(1)} collective-permute-done((bf16[64,4096]{1,0:T(8,128)(2,1)S(1)}, bf16[64,4096]{1,0:T(8,128)(2,1)S(1)}, u32[]{:S(2)}, u32[]{:S(2)}) %collective-permute-start.2) | collective-permute-done | bytes 524320 | tf_op jit(solution)/shard_map/ppermute | solution.py:48
  125.5 2.5 collective-permute-start.4
  128.0 12.2 %collective-permute-start.5 = (bf16[64,4096]{1,0:T(8,128)(2,1)S(1)}, bf16[64,4096]{1,0:T(8,128)(2,1)S(1)}, u32[]{:S(2)}, u32[]{:S(2)}) collective-permute-start(bf16[64,4096]{1,0:T(8,128)(2,1)S(1)} %collective-permute-done.3), channel_id=1, source_target_pairs={{0,7},{1,0},{2,1},{3,2},{4,3},{5,4},{6,5},{7,6},{8,15},{9,8},{10,9... | collective-permute-start | bytes 1572872 | tf_op jit(solution)/shard_map/ppermute | solution.py:53
  140.2 0.8 constant_dynamic-update-slice_fusion.4
  141.1 0.8 constant_dynamic-update-slice_fusion.3
  141.9 7.6 %collective-permute-done.4 = bf16[64,4096]{1,0:T(8,128)(2,1)S(1)} collective-permute-done((bf16[64,4096]{1,0:T(8,128)(2,1)S(1)}, bf16[64,4096]{1,0:T(8,128)(2,1)S(1)}, u32[]{:S(2)}, u32[]{:S(2)}) %collective-permute-start.4) | collective-permute-done | bytes 524320 | tf_op jit(solution)/shard_map/ppermute | solution.py:48
  149.5 3.0 collective-permute-start.6
  152.5 0.8 constant_dynamic-update-slice_fusion.2
  153.3 0.8 constant_dynamic-update-slice_fusion.1
  154.1 11.4 %collective-permute-done.6 = bf16[64,4096]{1,0:T(8,128)(2,1)S(1)} collective-permute-done((bf16[64,4096]{1,0:T(8,128)(2,1)S(1)}, bf16[64,4096]{1,0:T(8,128)(2,1)S(1)}, u32[]{:S(2)}, u32[]{:S(2)}) %collective-permute-start.6) | collective-permute-done | bytes 524320 | tf_op jit(solution)/shard_map/ppermute | solution.py:48
  165.5 0.8 constant_dynamic-update-slice_fusion
  166.4 25.4 %fusion.3 = f32[512,4096]{1,0:T(8,128)} fusion(bf16[512,4096]{1,0:T(8,128)(2,1)} %constant_dynamic-update-slice_fusion, bf16[4096,2048]{0,1:T(8,128)(2,1)} %get-tuple-element.15, bf16[4096,2048]{0,1:T(8,128)(2,1)} %get-tuple-element.16), kind=kOutput, calls=%fused_computation.7 | convolution fusion | flops 17246978048 | bytes 46137344 | tf_op jit(solution)/shard_map/dot_general | solution.py:58
  191.7 6.2 broadcast_in_dim.11
  197.9 19.7 %fusion.10 = f32[512,2048]{1,0:T(8,128)} fusion(bf16[512,4096]{1,0:T(8,128)(2,1)} %all-gather.3.cloned.1.call-done, bf16[2048,4096]{1,0:T(8,128)(2,1)} %param.12, bf16[256,8,32,128]{3,2,1,0:T(8,128)(2,1)} %bitcast.46), kind=kOutput, calls=%fused_computation.21 | convolution fusion | flops 8598323200 | bytes 41943040 | tf_op jit(solution)/shard_map/dot_general | solution.py:72
  217.6 0.0 all-gather.5.cloned.1.call-start
  217.7 0.7 all-gather.5.cloned.1.call-update
  218.4 0.2 reduce-scatter.3.cloned.1.call-start
  218.6 47.7 %all-reduce.3.cloned.1.call-done = (f32[512,4096]{1,0:T(8,128)}, f32[512,2048]{1,0:T(8,128)}) async-done(((f32[512,4096]{1,0:T(8,128)}, f32[512,2048]{1,0:T(8,128)}), (f32[512,4096]{1,0:T(8,128)}, f32[512,2048]{1,0:T(8,128)})) %all-reduce.3.cloned.1.call-update) | async-done | bytes 12582928 | tf_op jit(solution)/shard_map/psum | solution.py:58
  266.3 7.6 %multiply_convert_fusion.2 = (bf16[512,2048]{1,0:T(8,128)(2,1)}, bf16[512,2048]{1,0:T(8,128)(2,1)}, bf16[512,2048]{1,0:T(8,128)(2,1)S(1)}) fusion(f32[512,2048]{1,0:T(8,128)} %get-tuple-element.11, f32[512,4096]{1,0:T(8,128)} %get-tuple-element.10), kind=kLoop, calls=%fused_computation.17 | loop fusion | flops 15728640 | bytes 18874368 | tf_op jit(solution)/shard_map/convert_element_type | solution.py:80
  273.9 17.7 %fusion.5 = f32[512,4096]{1,0:T(8,128)} fusion(bf16[512,2048]{1,0:T(8,128)(2,1)S(1)} %get-tuple-element.14, bf16[2048,4096]{1,0:T(8,128)(2,1)} %param.12, bf16[256,8,32,128]{3,2,1,0:T(8,128)(2,1)} %bitcast.47), kind=kOutput, calls=%fused_computation.12 | convolution fusion | flops 8598323200 | bytes 44040192 | tf_op jit(solution)/shard_map/dot_general | solution.py:66
  291.7 0.0 reduce-scatter.5.cloned.1.call-start
  291.7 27.1 %fusion.2 = f32[512,4096]{1,0:T(8,128)} fusion(bf16[4096,2048]{0,1:T(8,128)(2,1)} %get-tuple-element.15, bf16[4096,2048]{0,1:T(8,128)(2,1)} %get-tuple-element.16, bf16[512,2048]{1,0:T(8,128)(2,1)} %get-tuple-element.13, bf16[512,2048]{1,0:T(8,128)(2,1)} %get-tuple-element.12), kind=kOutput, calls=%fused_computation.6 | convolution fusion | flops 17255366656 | bytes 46137344 | tf_op jit(solution)/shard_map/dot_general | solution.py:85
  318.9 24.2 %all-gather.5.cloned.1.call-done = bf16[512,4096]{1,0:T(8,128)(2,1)} async-done(((bf16[64,4096]{1,0:T(8,128)(2,1)}), bf16[512,4096]{1,0:T(8,128)(2,1)}) %all-gather.5.cloned.1.call-update) | async-done | bytes 4194320 | tf_op jit(solution)/shard_map/all_gather | solution.py:92
  343.1 22.4 %fusion.1 = bf16[4096,2048]{0,1:T(8,128)(2,1)} fusion(bf16[512,2048]{1,0:T(8,128)(2,1)} %get-tuple-element.12, bf16[512,4096]{1,0:T(8,128)(2,1)} %all-gather.5.cloned.1.call-done, bf16[256,8,32,128]{3,2,1,0:T(8,128)(2,1)} %bitcast.45), kind=kOutput, calls=%fused_computation.4 | convolution fusion | flops 8615100416 | bytes 39845888 | tf_op jit(solution)/shard_map/dot_general | solution.py:19
  365.5 22.5 %copy.16 = bf16[4096,2048]{1,0:T(8,128)(2,1)} copy(bf16[4096,2048]{0,1:T(8,128)(2,1)} %fusion.1) | data formatting | bytes 33554432
  388.0 22.9 %fusion = bf16[4096,2048]{0,1:T(8,128)(2,1)} fusion(bf16[512,2048]{1,0:T(8,128)(2,1)} %get-tuple-element.13, bf16[512,4096]{1,0:T(8,128)(2,1)} %all-gather.5.cloned.1.call-done, bf16[256,8,32,128]{3,2,1,0:T(8,128)(2,1)} %bitcast.43), kind=kOutput, calls=%fused_computation.2 | convolution fusion | flops 8615100416 | bytes 39845888 | tf_op jit(solution)/shard_map/dot_general | solution.py:19
  410.9 22.5 %copy.17 = bf16[4096,2048]{1,0:T(8,128)(2,1)} copy(bf16[4096,2048]{0,1:T(8,128)(2,1)} %fusion) | data formatting | bytes 33554432
  433.4 22.5 %multiply_convert_fusion = bf16[2048,4096]{1,0:T(8,128)(2,1)} fusion(bf16[512,2048]{1,0:T(8,128)(2,1)S(1)} %get-tuple-element.14, bf16[512,4096]{1,0:T(8,128)(2,1)} %all-gather.3.cloned.1.call-done, bf16[256,8,32,128]{3,2,1,0:T(8,128)(2,1)} %bitcast.48), kind=kOutput, calls=%fused_computation.5 | convolution fusion | flops 8615100416 | bytes 39845888 | tf_op jit(solution)/shard_map/dot_general | solution.py:19
  455.8 38.1 %reduce-scatter.3.cloned.1.call-done = f32[64,4096]{1,0:T(8,128)} async-done(((f32[512,4096]{1,0:T(8,128)}), f32[64,4096]{1,0:T(8,128)}) %reduce-scatter.3.cloned.1.call-update) | async-done | bytes 1048592 | tf_op jit(solution)/shard_map/reduce_scatter | solution.py:65
  493.9 2.1 convert_element_type.46
  496.0 149.9 %reduce-scatter.5.cloned.1.call-done = f32[64,4096]{1,0:T(8,128)} async-done(((f32[512,4096]{1,0:T(8,128)}), f32[64,4096]{1,0:T(8,128)}) %reduce-scatter.5.cloned.1.call-update) | async-done | bytes 1048592 | tf_op jit(solution)/shard_map/reduce_scatter | solution.py:84
  645.9 2.1 convert_element_type.49
  (21 shorter events, 0.1 us)
Async XLA Ops:
  7.2 184.6 %all-gather.3.cloned.1.call-start = ((), (), s32[]{:S(2)}) async-start(), calls=%async_computation.3 | async-start | bytes 4718592 | tf_op jit(solution)/shard_map/all_gather | solution.py:71
  7.2 95.9 %collective-permute-start = (bf16[64,4096]{1,0:T(8,128)(2,1)}, bf16[64,4096]{1,0:T(8,128)(2,1)S(1)}, u32[]{:S(2)}, u32[]{:S(2)}) collective-permute-start(bf16[64,4096]{1,0:T(8,128)(2,1)} %param.8), channel_id=1, source_target_pairs={{0,1},{1,2},{2,3},{3,4},{4,5},{5,6},{6,7},{7,0},{8,9},{9,10},{10,1... | collective-permute-start | bytes 1572872 | tf_op jit(solution)/shard_map/ppermute | solution.py:48
  10.2 93.0 %collective-permute-start.1 = (bf16[64,4096]{1,0:T(8,128)(2,1)}, bf16[64,4096]{1,0:T(8,128)(2,1)S(1)}, u32[]{:S(2)}, u32[]{:S(2)}) collective-permute-start(bf16[64,4096]{1,0:T(8,128)(2,1)} %param.8), channel_id=1, source_target_pairs={{0,7},{1,0},{2,1},{3,2},{4,3},{5,4},{6,5},{7,6},{8,15},{9,8},{10,9... | collective-permute-start | bytes 1572872 | tf_op jit(solution)/shard_map/ppermute | solution.py:53
  13.3 21.3 %copy-start.2 = (s32[32,16]{0,1:T(8,128)S(1)}, s32[32,16]{0,1:T(8,128)}, u32[]{:S(2)}) copy-start(s32[32,16]{0,1:T(8,128)} %param.14) | copy-start | bytes 6148
  13.3 253.0 %all-reduce.3.cloned.1.call-start = ((), (), s32[]{:S(2)}) async-start(), calls=%async_computation.6 | async-start | bytes 25165824 | tf_op jit(solution)/shard_map/psum | solution.py:58
  34.7 21.4 %copy-start.3 = (s32[32,16]{0,1:T(8,128)S(1)}, s32[32,16]{0,1:T(8,128)}, u32[]{:S(2)}) copy-start(s32[32,16]{0,1:T(8,128)} %param.13) | copy-start | bytes 6148
  59.0 10.8 %copy-start = (bf16[32,128,16,128]{1,0,3,2:T(8,128)(2,1)}, bf16[32,128,16,128]{1,0,3,2:T(8,128)(2,1)S(1)}, u32[]{:S(2)}) copy-start(bf16[32,128,16,128]{1,0,3,2:T(8,128)(2,1)S(1)} %broadcast_in_dim.10) | copy-start | bytes 50331652
  69.7 30.1 %copy-start.4 = (s32[16,32]{1,0:T(8,128)S(1)}, s32[16,32]{1,0:T(8,128)}, u32[]{:S(2)}) copy-start(s32[16,32]{1,0:T(8,128)} %param.15) | copy-start | bytes 6148
  69.7 32.6 %copy-start.1 = (bf16[64,4096]{1,0:T(8,128)(2,1)S(1)}, bf16[64,4096]{1,0:T(8,128)(2,1)}, u32[]{:S(2)}) copy-start(bf16[64,4096]{1,0:T(8,128)(2,1)} %param.8) | copy-start | bytes 1572868
  103.2 22.4 %collective-permute-start.2 = (bf16[64,4096]{1,0:T(8,128)(2,1)S(1)}, bf16[64,4096]{1,0:T(8,128)(2,1)S(1)}, u32[]{:S(2)}, u32[]{:S(2)}) collective-permute-start(bf16[64,4096]{1,0:T(8,128)(2,1)S(1)} %collective-permute-done), channel_id=1, source_target_pairs={{0,1},{1,2},{2,3},{3,4},{4,5},{5,6},{6,7},{7,0},{8,9},{9,10},{10,1... | collective-permute-start | bytes 1572872 | tf_op jit(solution)/shard_map/ppermute | solution.py:48
  103.2 24.8 %collective-permute-start.3 = (bf16[64,4096]{1,0:T(8,128)(2,1)S(1)}, bf16[64,4096]{1,0:T(8,128)(2,1)S(1)}, u32[]{:S(2)}, u32[]{:S(2)}) collective-permute-start(bf16[64,4096]{1,0:T(8,128)(2,1)S(1)} %collective-permute-done.1), channel_id=1, source_target_pairs={{0,7},{1,0},{2,1},{3,2},{4,3},{5,4},{6,5},{7,6},{8,15},{9,8},{10,9... | collective-permute-start | bytes 1572872 | tf_op jit(solution)/shard_map/ppermute | solution.py:53
  125.5 24.0 %collective-permute-start.4 = (bf16[64,4096]{1,0:T(8,128)(2,1)S(1)}, bf16[64,4096]{1,0:T(8,128)(2,1)S(1)}, u32[]{:S(2)}, u32[]{:S(2)}) collective-permute-start(bf16[64,4096]{1,0:T(8,128)(2,1)S(1)} %collective-permute-done.2), channel_id=1, source_target_pairs={{0,1},{1,2},{2,3},{3,4},{4,5},{5,6},{6,7},{7,0},{8,9},{9,10},{10,1... | collective-permute-start | bytes 1572872 | tf_op jit(solution)/shard_map/ppermute | solution.py:48
  128.0 25.3 %collective-permute-start.5 = (bf16[64,4096]{1,0:T(8,128)(2,1)S(1)}, bf16[64,4096]{1,0:T(8,128)(2,1)S(1)}, u32[]{:S(2)}, u32[]{:S(2)}) collective-permute-start(bf16[64,4096]{1,0:T(8,128)(2,1)S(1)} %collective-permute-done.3), channel_id=1, source_target_pairs={{0,7},{1,0},{2,1},{3,2},{4,3},{5,4},{6,5},{7,6},{8,15},{9,8},{10,9... | collective-permute-start | bytes 1572872 | tf_op jit(solution)/shard_map/ppermute | solution.py:53
  149.5 16.1 %collective-permute-start.6 = (bf16[64,4096]{1,0:T(8,128)(2,1)S(1)}, bf16[64,4096]{1,0:T(8,128)(2,1)S(1)}, u32[]{:S(2)}, u32[]{:S(2)}) collective-permute-start(bf16[64,4096]{1,0:T(8,128)(2,1)S(1)} %collective-permute-done.4), channel_id=1, source_target_pairs={{0,1},{1,2},{2,3},{3,4},{4,5},{5,6},{6,7},{7,0},{8,9},{9,10},{10,1... | collective-permute-start | bytes 1572872 | tf_op jit(solution)/shard_map/ppermute | solution.py:48
  217.6 125.4 %all-gather.5.cloned.1.call-start = ((), (), s32[]{:S(2)}) async-start(), calls=%async_computation.5 | async-start | bytes 4718592 | tf_op jit(solution)/shard_map/all_gather | solution.py:92
  218.4 275.5 %reduce-scatter.3.cloned.1.call-start = ((), (), s32[]{:S(2)}) async-start(), calls=%async_computation.2 | async-start | bytes 9437184 | tf_op jit(solution)/shard_map/reduce_scatter | solution.py:65
  291.7 354.2 %reduce-scatter.5.cloned.1.call-start = ((), (), s32[]{:S(2)}) async-start(), calls=%async_computation.4 | async-start | bytes 9437184 | tf_op jit(solution)/shard_map/reduce_scatter | solution.py:84
Sparse Core Ops, SparseCore 0:
  13.5 78.9 all-gather.2
  217.8 48.5 all-reduce.2
  268.5 74.5 all-gather.4
  346.5 147.3 reduce-scatter.2
  497.8 148.0 reduce-scatter.4
